TPU v7x, 32 devices: a whole 2x2x4 slice. The times are simulated.
32 devices in a mesh: row: 4 (over y, x), col: 8 (over z, core).
Axes of the slice: x: 2, y: 2, z: 4, core: 2. Of those that a mesh axis runs over, the one named last changes fastest.
Arguments:
- tokens: bfloat16 [1024, 2304], P('row', 'col'), may hold values from -6 to 6
- gate_weight: bfloat16 [8, 2304, 5760], P(None, 'col', 'row'), may hold values from -0.125 to 0.125
- up_weight: bfloat16 [8, 2304, 5760], P(None, 'col', 'row'), may hold values from -0.125 to 0.125
- down_weight: bfloat16 [8, 5760, 2304], P(None, 'row', 'col'), may hold values from -0.078125 to 0.078125
- route_ids: int32 [1024, 2], replicated, may hold values from 0 to 7, all different within a row; in each aligned block of 1024 rows (0 to 1023, 1024 to 2047, ...) at most 512 rows name the same one
- route_weight: float32 [1024, 2], replicated, may hold values from 0.2 to 1
- prefill_cache: bfloat16 [2, 256, 16, 2304], P(None, ('row', 'col')), may hold values from -6 to 6
- dest_col: int32 [4, 8, 8], P('row'), may hold values from 0 to 7, as said below
- dest_slot: int32 [4, 8, 8], P('row'), may hold values from 0 to 7, as said below
- pages_used: int32 [4, 8], P('row'), may hold values from 2 to 8, as said below
Outputs:
- mixed: bfloat16 [1024, 2304], P('row', 'col')
- decode_cache: bfloat16 [2, 256, 16, 2304], P(None, ('row', 'col'))
Inputs may be any that keep to these rules, and one draw needn't show every extreme that they name: `route_ids`: each token names two different experts; no expert is named by more than 512 tokens, a bound that some block reaches. For every device (r, c), dest_col[r, c, :] names each col index exactly 1 times. For every r and col index c2, the page slots of row r with dest_col = c2 carry distinct dest_slot values, so they fill all 8 slots of device (r, c2). The live slots of a device are its first pages_used slots; some device has all 8 live.
All inputs are finite; a program needn't handle non-finite values.
Results may differ from a plain program's by a relative error of at most 0.03.
Values may be sent and summed in bfloat16 or wider, within the bound.
A program may use at most 192 MiB of HBM per device.

v0:
```python
import jax
import jax.numpy as jnp
from jax import lax
from jax.sharding import PartitionSpec as P


def aligned_apply(slot_rows, weights):
    experts = weights.shape[0]
    shaped = slot_rows.reshape(experts, -1, slot_rows.shape[1])
    product = jnp.einsum("ecd,edf->ecf", shaped, weights, preferred_element_type=jnp.float32)
    return product.reshape(-1, weights.shape[2])


def move_pages(prefill_cache, dest_col, dest_slot, pages_used):
    col_devices = lax.axis_size("col")
    own_index = lax.axis_index("col")
    slot_count = prefill_cache.shape[1]
    per_peer = slot_count // col_devices
    dest_table = dest_col[0]
    targets = dest_slot[0]
    page_index = jnp.arange(slot_count, dtype=jnp.int32)
    same_dest = dest_table[:, :, None] == dest_table[:, None, :]
    earlier = page_index[None, :] < page_index[:, None]
    dest_rank = jnp.sum((same_dest & earlier[None]).astype(jnp.int32), axis=2)
    send_order = lax.dynamic_index_in_dim(
        dest_table * per_peer + dest_rank, own_index, 0, keepdims=False
    )
    inverse = jnp.zeros((slot_count,), jnp.int32).at[send_order].set(page_index)
    own_used = lax.dynamic_index_in_dim(pages_used[0], own_index, 0, keepdims=False)
    is_live = page_index < own_used
    masked_pages = jnp.where(
        is_live[None, :, None, None], prefill_cache, jnp.zeros((), prefill_cache.dtype)
    )
    received = lax.all_to_all(
        masked_pages[:, inverse], "col", split_axis=1, concat_axis=1, tiled=True
    )
    senders = jnp.arange(col_devices, dtype=jnp.int32)[:, None]
    arrival = jnp.where(dest_table == own_index, senders * per_peer + dest_rank, slot_count)
    slot_of_arrival = (
        jnp.zeros((slot_count + 1,), jnp.int32)
        .at[arrival.reshape(-1)]
        .set(targets.reshape(-1))[:slot_count]
    )
    source_of_slot = jnp.zeros((slot_count,), jnp.int32).at[slot_of_arrival].set(page_index)
    return received[:, source_of_slot]


def shards(
    tokens,
    gate_weight,
    up_weight,
    down_weight,
    route_ids,
    route_weight,
    prefill_cache,
    dest_col,
    dest_slot,
    pages_used,
):
    decode_cache = move_pages(prefill_cache, dest_col, dest_slot, pages_used)
    gathered = lax.all_gather(tokens, "row", axis=0, tiled=True)
    token_count = route_ids.shape[0]
    assignments = token_count * 2
    capacity = token_count // 2
    experts = gate_weight.shape[0]
    flat_expert = route_ids.reshape(-1)
    labels = jnp.arange(experts, dtype=jnp.int32)
    assign_index = jnp.arange(assignments, dtype=jnp.int32)
    paired = jnp.concatenate([gate_weight, up_weight], axis=2)
    onehot = (flat_expert[:, None] == labels[None, :]).astype(jnp.int32)
    position = jnp.sum(jnp.cumsum(onehot, axis=0) * onehot, axis=1) - 1
    slot_of_assign = flat_expert * capacity + position
    row_assign = (
        jnp.full((experts * capacity,), assignments, jnp.int32).at[slot_of_assign].set(assign_index)
    )
    row_token = row_assign // 2
    padded_tokens = jnp.concatenate(
        [gathered, jnp.zeros((1, gathered.shape[1]), gathered.dtype)], axis=0
    )
    slot_rows = padded_tokens[row_token]
    weights_flat = jnp.concatenate([route_weight.reshape(-1), jnp.zeros((1,), jnp.float32)])
    row_weight = weights_flat[row_assign]
    partial_sums = aligned_apply(slot_rows, paired)
    summed = lax.psum_scatter(
        partial_sums.astype(jnp.bfloat16), "col", scatter_dimension=0, tiled=True
    ).astype(jnp.float32)
    share_rows = summed.shape[0]
    hidden_width = gate_weight.shape[2]
    own_weight = lax.dynamic_slice_in_dim(
        row_weight, lax.axis_index("col") * share_rows, share_rows, 0
    )
    hidden = (
        own_weight[:, None] * jax.nn.silu(summed[:, :hidden_width]) * summed[:, hidden_width:]
    ).astype(jnp.bfloat16)
    hidden_all = lax.all_gather(hidden, "col", axis=0, tiled=True)
    down_rows = aligned_apply(hidden_all, down_weight)
    pair_slots = slot_of_assign.reshape(token_count, 2)
    per_token = down_rows[pair_slots[:, 0]] + down_rows[pair_slots[:, 1]]
    mixed = lax.psum_scatter(per_token.astype(jnp.bfloat16), "row", scatter_dimension=0, tiled=True)
    return (mixed, decode_cache)


def solution(mesh):
    in_specs = (
        P("row", "col"),
        P(None, "col", "row"),
        P(None, "col", "row"),
        P(None, "row", "col"),
        P(),
        P(),
        P(None, ("row", "col"), None, None),
        P("row", None, None),
        P("row", None, None),
        P("row", None),
    )
    out_specs = (P("row", "col"), P(None, ("row", "col"), None, None))
    return jax.shard_map(shards, mesh=mesh, in_specs=in_specs, out_specs=out_specs, check_vma=False)
```

profile of v0, /device:TPU:0, one launch (start us, length us, event | category | flops | bytes accessed | tf_op | source)
XLA Modules:
  0.0 563.2 jit_solution(17477042519855468694)
XLA Ops:
  7.2 0.9 copy.45
  8.7 2.3 reduce-window.6
  11.6 0.5 sub.17
  12.2 0.3 mul.40
  12.5 8.1 %scatter_custom_fusion = s32[4096]{0:T(1024)S(1)} fusion(s32[2048]{0:T(1024)S(1)} %bitcast.43, s32[2048]{0:T(1024)S(1)} %iota.33, s32[]{:T(128)} %constant.20.clone.1), kind=kCustom, calls=%fused_computation.45 | custom fusion | bytes 16388 | tf_op jit(solution)/shard_map/scatter | solution.py:74
  20.8 12.7 %all_gather.6 = bf16[1024,288]{1,0:T(8,128)(2,1)S(1)} all-gather(bf16[256,288]{1,0:T(8,128)(2,1)S(1)} %copy.48), channel_id=1, replica_groups=mesh['row'=4,'col'=8] {'row'}, dimensions={0}, use_global_device_ids=true | all-gather | bytes 737280 | tf_op jit(solution)/shard_map/all_gather | solution.py:61
  33.6 17.0 %gather_fusion.1 = bf16[4096,288]{1,0:T(8,128)(2,1)} fusion(bf16[1025,288]{1,0:T(8,128)(2,1)S(1)} %concatenate.10, s32[4096]{0:T(1024)S(1)} %get-tuple-element.15), kind=kCustom, calls=%fused_computation.1 | custom fusion | bytes 4734976 | tf_op jit(solution)/shard_map/gather | solution.py:80
  50.6 37.7 %convolution_convert_fusion = bf16[8,512,2880]{1,2,0:T(8,128)(2,1)} fusion(bf16[8,512,288]{2,1,0:T(8,128)(2,1)} %bitcast.39, bf16[8,288,1440]{2,1,0:T(8,128)(2,1)} %param.12, bf16[8,288,1440]{2,1,0:T(8,128)(2,1)} %param.11), kind=kOutput, calls=%fused_computation.10 | convolution fusion | flops 6833111040 | bytes 39223296 | tf_op jit(solution)/shard_map/ecd,edf->ecf/dot_general | solution.py:10
  88.3 32.0 %copy.50 = bf16[8,512,2880]{2,1,0:T(8,128)(2,1)} copy(bf16[8,512,2880]{1,2,0:T(8,128)(2,1)} %convolution_convert_fusion) | data formatting | bytes 47185920 | tf_op jit(solution)/shard_map/convert_element_type | solution.py:85
  120.5 0.4 copy-done.4
  121.5 23.0 %gather_fusion = f32[4096]{0:T(1024)S(1)} fusion(f32[2049]{0:T(1024)S(1)} %pad_maximum_fusion, s32[4096]{0:T(1024)S(1)} %get-tuple-element.14), kind=kCustom, calls=%fused_computation | custom fusion | bytes 49152 | tf_op jit(solution)/shard_map/gather | solution.py:82
  144.6 213.5 %reduce-scatter.3.cloned.1.call-done = bf16[512,2880]{1,0:T(8,128)(2,1)} async-done(((bf16[4096,2880]{1,0:T(8,128)(2,1)}), bf16[512,2880]{1,0:T(8,128)(2,1)}) %reduce-scatter.3.cloned.1.call-update) | async-done | bytes 2949136 | tf_op jit(solution)/shard_map/reduce_scatter | solution.py:84
  358.1 2.3 convert_element_type.26
  360.4 2.4 fusion.3
  363.4 0.6 constant_dynamic-slice_fusion
  364.0 0.6 scatter_custom_fusion.1
  364.6 0.8 scatter_custom_fusion.2
  365.4 0.7 iota_compare_fusion.3
  366.2 1.6 gather_fusion.4
  367.9 4.3 all-to-all-start
  372.2 0.5 fusion.5
  372.7 130.4 %all-gather.2.cloned.1.call-done = bf16[4096,1440]{1,0:T(8,128)(2,1)} async-done(((bf16[512,1440]{1,0:T(8,128)(2,1)}), bf16[4096,1440]{1,0:T(8,128)(2,1)}) %all-gather.2.cloned.1.call-update) | async-done | bytes 11796496 | tf_op jit(solution)/shard_map/all_gather | solution.py:95
  503.1 13.3 %fusion.25 = f32[8,512,288]{2,1,0:T(8,128)} fusion(bf16[8,1440,288]{1,2,0:T(8,128)(2,1)} %param.13, bf16[8,512,1440]{2,1,0:T(8,128)(2,1)} %bitcast.44), kind=kOutput, calls=%fused_computation.73 | convolution fusion | flops 3397386240 | bytes 23150592 | tf_op jit(solution)/shard_map/reshape | solution.py:11
  516.3 6.6 %gather_fusion.3 = f32[1024,288]{1,0:T(8,128)S(1)} fusion(f32[4096,288]{1,0:T(8,128)} %bitcast.35, s32[1024]{0:T(1024)S(1)} %get-tuple-element.20), kind=kCustom, calls=%fused_computation.3 | custom fusion | bytes 2363392 | tf_op jit(solution)/shard_map/gather | solution.py:98
  522.9 6.6 %gather_fusion.2 = f32[1024,288]{1,0:T(8,128)S(1)} fusion(f32[4096,288]{1,0:T(8,128)} %bitcast.36, s32[1024]{0:T(1024)S(1)} %get-tuple-element.21), kind=kCustom, calls=%fused_computation.2 | custom fusion | bytes 2363392 | tf_op jit(solution)/shard_map/gather | solution.py:98
  529.5 1.0 add_convert_fusion
  530.5 0.6 scatter_custom_fusion.3
  531.2 1.3 copy.56
  532.5 0.6 gather_fusion.5
  533.1 1.1 copy.58
  534.2 20.7 %reduce-scatter.5.cloned.1.call-done = bf16[256,288]{1,0:T(8,128)(2,1)} async-done(((bf16[1024,288]{1,0:T(8,128)(2,1)}), bf16[256,288]{1,0:T(8,128)(2,1)}) %reduce-scatter.5.cloned.1.call-update) | async-done | bytes 147472 | tf_op jit(solution)/shard_map/reduce_scatter | solution.py:99
  554.9 1.7 copy.57
  (53 shorter events, 3.2 us)
Async XLA Ops:
  7.2 356.2 %copy-start = (s32[1,8]{1,0:T(1,128)S(1)}, s32[1,8]{1,0:T(1,128)}, u32[]{:S(2)}) copy-start(s32[1,8]{1,0:T(1,128)} %param.19) | copy-start | bytes 100
  7.2 13.5 %copy-start.2 = (bf16[256,288]{0,1:T(8,128)(2,1)S(1)}, bf16[256,288]{0,1:T(8,128)(2,1)}, u32[]{:S(2)}) copy-start(bf16[256,288]{0,1:T(8,128)(2,1)} %param.10) | copy-start | bytes 442372
  7.2 350.9 %reduce-scatter.3.cloned.1.call-start = ((), (), s32[]{:S(2)}) async-start(), calls=%async_computation.3 | async-start | bytes 27131904 | tf_op jit(solution)/shard_map/reduce_scatter | solution.py:84
  120.3 0.7 copy-start.4
  120.3 382.8 %all-gather.2.cloned.1.call-start = ((), (), s32[]{:S(2)}) async-start(), calls=%async_computation.4 | async-start | bytes 14155776 | tf_op jit(solution)/shard_map/all_gather | solution.py:95
  360.3 2.5 copy-start.3
  360.3 3.0 copy-start.5
  360.3 5.7 %copy-start.1 = (bf16[2,8,16,2304]{3,2,1,0:T(8,128)(2,1)S(1)}, bf16[2,8,16,2304]{3,2,1,0:T(8,128)(2,1)}, u32[]{:S(2)}) copy-start(bf16[2,8,16,2304]{3,2,1,0:T(8,128)(2,1)} %param.16) | copy-start | bytes 3538948
  367.9 163.3 %all-to-all-start = ((bf16[2,8,16,2304]{3,2,0,1:T(8,128)(2,1)}), bf16[2,8,16,2304]{3,2,0,1:T(8,128)(2,1)}, u32[]{:S(2)}, u32[]{:S(2)}) async-start(bf16[2,8,16,2304]{3,2,0,1:T(8,128)(2,1)} %bitcast.10), calls=%async_computation.2 | async-start | bytes 2359296 | tf_op jit(solution)/shard_map/all_to_all | solution.py:34
  372.1 182.8 %reduce-scatter.5.cloned.1.call-start = ((), (), s32[]{:S(2)}) async-start(), calls=%async_computation.5 | async-start | bytes 983040 | tf_op jit(solution)/shard_map/reduce_scatter | solution.py:99
Sparse Core Ops, SparseCore 0:
  120.4 237.6 reduce-scatter.2
  362.9 140.1 all-gather.1
  530.6 24.2 reduce-scatter.4
where the time goes:
time: 564 us; the launch traced here: 563 us
  waiting for transfers between devices  365 us (65%)
  local copies, waits for them, and re-layouts  106 us (19%)
  matrix products  51 us (9%)
  between operations  14.1 us (2%)
  blocking collectives  12.7 us (2%)
  other arithmetic  10 us (2%)
    reduce_scatter x1, waiting for transfers between devices, shards(): lax.psum_scatter(partial_sums.astype(jnp.bfloat16), 'col', scatter_dimens...  213 us
    all_gather x1, waiting for transfers between devices, shards(): hidden_all = lax.all_gather(hidden, 'col', axis=0, tiled=True)  130 us
    dot_general x1, matrix products, aligned_apply(): jnp.einsum('ecd,edf->ecf', shaped, weights, preferred_element_type=jnp.fl...  37.7 us
    convert_element_type x1, local copies, waits for them, and re-layouts, shards(): partial_sums.astype(jnp.bfloat16)  32 us
    gather x1, local copies, waits for them, and re-layouts, shards(): row_weight = weights_flat[row_assign]  23 us
    reduce_scatter x1, waiting for transfers between devices, shards(): lax.psum_scatter(per_token.astype(jnp.bfloat16), 'row', scatter_dimension...  20.7 us
    gather x1, local copies, waits for them, and re-layouts, shards(): slot_rows = padded_tokens[row_token]  17 us
    reshape x1, matrix products, aligned_apply(): return product.reshape(-1, weights.shape[2])  13.3 us
  transfers between devices with their start and end apart: 4, of which 3 were waited for; matrix products, arithmetic and copies ran while one was open for 11% of the time, Pallas kernels for 0%

commit v1 on v0

v1 whole, which is shorter than its diff:
```python
import jax
import jax.numpy as jnp
from jax import lax
from jax.experimental import pallas as pl
from jax.experimental.pallas import tpu as pltpu
from jax.sharding import PartitionSpec as P

TILE = 256
VMEM_BYTES = 48 * 1024 * 1024


def sorted_places(route_ids, experts):
    tokens = route_ids.shape[0]
    group = 128
    labels = jnp.arange(experts, dtype=jnp.int32)
    onehot = (route_ids[:, :, None] == labels).astype(jnp.float32)
    per_token = jnp.sum(onehot, axis=1).reshape(tokens // group, group, experts)
    below = jnp.tril(jnp.ones((group, group), jnp.bfloat16), -1)
    within = jnp.einsum(
        "ij,bje->bie", below, per_token.astype(jnp.bfloat16), preferred_element_type=jnp.float32
    )
    totals = jnp.sum(per_token, axis=1)
    blocks = jnp.arange(tokens // group)
    earlier = jnp.sum(jnp.where(blocks[:, None, None] > blocks[None, :, None], totals[None], 0.0), axis=1)
    counts = jnp.sum(totals, axis=0)
    starts = jnp.sum(jnp.where(labels[:, None] > labels[None, :], counts[None, :], 0.0), axis=1)
    base = (within + earlier[:, None, :] + starts).reshape(tokens, experts)
    places = jnp.sum(onehot * base[:, None, :], axis=2).astype(jnp.int32)
    starts = starts.astype(jnp.int32)
    return places, starts, starts + counts.astype(jnp.int32)


def step_table(starts, ends, rows):
    experts = starts.shape[0]
    tiles = rows // TILE
    labels = jnp.arange(experts, dtype=jnp.int32)
    spans = jnp.where(ends > starts, (ends - 1) // TILE - starts // TILE + 1, 0)
    after = jnp.sum(jnp.where(labels[:, None] >= labels[None, :], spans[None, :], 0), axis=1)
    step = jnp.arange(tiles + experts - 1, dtype=jnp.int32)
    expert = jnp.minimum(jnp.sum((after[None, :] <= step[:, None]).astype(jnp.int32), axis=1), experts - 1)
    chosen = expert[:, None] == labels[None, :]

    def pick(table):
        return jnp.sum(jnp.where(chosen, table[None, :], 0), axis=1)

    live = step < after[experts - 1]
    tile = jnp.where(live, pick(starts) // TILE + step - pick(after - spans), tiles - 1)
    low = jnp.where(live, jnp.maximum(pick(starts), tile * TILE), 0)
    high = jnp.where(live, jnp.minimum(pick(ends), tile * TILE + TILE), 0)
    return tile, expert, low, high


def up_kernel(tile, expert, low, high, first, second, tokens, gate, up, out):
    s = pl.program_id(0)
    place = tile[s] * TILE + lax.broadcasted_iota(jnp.int32, (TILE, 1), 0)
    mask = (place >= low[s]) & (place < high[s])
    pick = (first[...] == place) | (second[...] == place)
    rows = jnp.dot(
        jnp.where(pick, 1.0, 0.0).astype(jnp.bfloat16), tokens[...], preferred_element_type=jnp.float32
    ).astype(jnp.bfloat16)
    for i, weight in enumerate((gate, up)):
        product = jnp.dot(rows, weight[0], preferred_element_type=jnp.float32)
        out[i] = jnp.where(mask, product, out[i].astype(jnp.float32)).astype(jnp.bfloat16)


def up_products(table, places, tokens, gate_weight, up_weight):
    count = tokens.shape[0]
    rows = 2 * count
    _, depth, width = gate_weight.shape
    whole = lambda s, *_: (0, 0)
    weight = pl.BlockSpec((1, depth, width), lambda s, tile, expert, *_: (expert[s], 0, 0))
    return pl.pallas_call(
        up_kernel,
        out_shape=jax.ShapeDtypeStruct((2, rows, width), jnp.bfloat16),
        grid_spec=pltpu.PrefetchScalarGridSpec(
            num_scalar_prefetch=4,
            grid=(table[0].shape[0],),
            in_specs=[
                pl.BlockSpec((1, count), whole),
                pl.BlockSpec((1, count), whole),
                pl.BlockSpec((count, depth), whole),
                weight,
                weight,
            ],
            out_specs=pl.BlockSpec((2, TILE, width), lambda s, tile, *_: (0, tile[s], 0)),
        ),
        compiler_params=pltpu.CompilerParams(vmem_limit_bytes=VMEM_BYTES),
    )(*table, places[:, 0].reshape(1, -1), places[:, 1].reshape(1, -1), tokens, gate_weight, up_weight)


def down_kernel(tile, expert, low, high, first, second, hidden, weight, out, total):
    s = pl.program_id(0)

    @pl.when(s == 0)
    def _():
        total[...] = jnp.zeros_like(total)

    place = tile[s] * TILE + lax.broadcasted_iota(jnp.int32, (1, TILE), 1)
    mask = (place >= low[s]) & (place < high[s])
    place = jnp.where(mask, place, -1)
    pick = (first[...] == place) | (second[...] == place)
    product = jnp.dot(hidden[...], weight[0], preferred_element_type=jnp.float32).astype(jnp.bfloat16)
    total[...] += jnp.dot(
        jnp.where(pick, 1.0, 0.0).astype(jnp.bfloat16), product, preferred_element_type=jnp.float32
    )

    @pl.when(s == pl.num_programs(0) - 1)
    def _():
        out[...] = total[...].astype(jnp.bfloat16)


def down_products(table, places, hidden, down_weight):
    count = places.shape[0]
    _, width, depth = down_weight.shape
    whole = lambda s, *_: (0, 0)
    return pl.pallas_call(
        down_kernel,
        out_shape=jax.ShapeDtypeStruct((count, depth), jnp.bfloat16),
        grid_spec=pltpu.PrefetchScalarGridSpec(
            num_scalar_prefetch=4,
            grid=(table[0].shape[0],),
            in_specs=[
                pl.BlockSpec((count, 1), whole),
                pl.BlockSpec((count, 1), whole),
                pl.BlockSpec((TILE, width), lambda s, tile, *_: (tile[s], 0)),
                pl.BlockSpec((1, width, depth), lambda s, tile, expert, *_: (expert[s], 0, 0)),
            ],
            out_specs=pl.BlockSpec((count, depth), whole),
            scratch_shapes=[pltpu.VMEM((count, depth), jnp.float32)],
        ),
        compiler_params=pltpu.CompilerParams(vmem_limit_bytes=VMEM_BYTES),
    )(*table, places[:, 0:1], places[:, 1:2], hidden, down_weight)


def page_kernel(source, keep, page, out):
    live = jnp.broadcast_to(keep[pl.program_id(0)] > 0, out.shape)
    out[...] = jnp.where(live, page[...], jnp.zeros_like(page))


def take_pages(cache, source, keep):
    block = (cache.shape[0], 1, *cache.shape[2:])
    return pl.pallas_call(
        page_kernel,
        out_shape=jax.ShapeDtypeStruct(cache.shape, cache.dtype),
        grid_spec=pltpu.PrefetchScalarGridSpec(
            num_scalar_prefetch=2,
            grid=(source.shape[0],),
            in_specs=[pl.BlockSpec(block, lambda p, source, keep: (0, source[p], 0, 0))],
            out_specs=pl.BlockSpec(block, lambda p, source, keep: (0, p, 0, 0)),
        ),
    )(source, keep, cache)


def move_pages(prefill_cache, dest_col, dest_slot, pages_used):
    col_devices = lax.axis_size("col")
    own = lax.axis_index("col")
    slots = prefill_cache.shape[1]
    per_peer = slots // col_devices
    page = jnp.arange(slots, dtype=jnp.int32)
    peers = jnp.arange(col_devices, dtype=jnp.int32)
    table = dest_col[0]
    earlier = (table[:, :, None] == table[:, None, :]) & (page[None, :] < page[:, None])[None]
    order = jnp.sum(earlier.astype(jnp.int32), axis=2)
    sends = table * per_peer + order
    is_own = (peers == own)[:, None]
    own_sends = jnp.sum(jnp.where(is_own, sends, 0), axis=0)
    own_used = jnp.sum(jnp.where(peers == own, pages_used[0], 0))
    source = jnp.sum(jnp.where(own_sends[None, :] == page[:, None], page[None, :], 0), axis=1)
    received = lax.all_to_all(
        take_pages(prefill_cache, source, (source < own_used).astype(jnp.int32)),
        "col",
        split_axis=1,
        concat_axis=1,
        tiled=True,
    )
    arrival = peers[:, None] * per_peer + order
    mine = (table == own)[None] & (dest_slot[0][None] == page[:, None, None])
    origin = jnp.sum(jnp.where(mine, arrival[None], 0), axis=(1, 2))
    return take_pages(received, origin, jnp.ones_like(origin))


def shards(
    tokens,
    gate_weight,
    up_weight,
    down_weight,
    route_ids,
    route_weight,
    prefill_cache,
    dest_col,
    dest_slot,
    pages_used,
):
    rows = 2 * route_ids.shape[0]
    gathered = lax.all_gather(tokens, "row", axis=0, tiled=True)
    decode_cache = move_pages(prefill_cache, dest_col, dest_slot, pages_used)
    places, starts, ends = sorted_places(route_ids, gate_weight.shape[0])
    table = step_table(starts, ends, rows)
    partial_sums = up_products(table, places, gathered, gate_weight, up_weight)
    summed = lax.psum_scatter(partial_sums, "col", scatter_dimension=1, tiled=True).astype(jnp.float32)
    share = summed.shape[1]
    own_rows = lax.axis_index("col") * share + jnp.arange(share, dtype=jnp.int32)
    own_weight = jnp.sum(
        jnp.where(own_rows[:, None, None] == places[None], route_weight[None], 0.0), axis=(1, 2)
    )
    hidden = (own_weight[:, None] * jax.nn.silu(summed[0]) * summed[1]).astype(jnp.bfloat16)
    hidden_all = lax.all_gather(hidden, "col", axis=0, tiled=True)
    per_token = down_products(table, places, hidden_all, down_weight)
    mixed = lax.psum_scatter(per_token, "row", scatter_dimension=0, tiled=True)
    return (mixed, decode_cache)


def solution(mesh):
    in_specs = (
        P("row", "col"),
        P(None, "col", "row"),
        P(None, "col", "row"),
        P(None, "row", "col"),
        P(),
        P(),
        P(None, ("row", "col"), None, None),
        P("row", None, None),
        P("row", None, None),
        P("row", None),
    )
    out_specs = (P("row", "col"), P(None, ("row", "col"), None, None))
    return jax.shard_map(shards, mesh=mesh, in_specs=in_specs, out_specs=out_specs, check_vma=False)
```

time: 564 us -> 328 us (0.58)
  waiting for transfers between devices: 365 us -> 207 us
  local copies, waits for them, and re-layouts: 106 us -> 19.8 us
  Pallas kernels: 0 us -> 59.4 us
  matrix products: 51 us -> 0.2 us
    reduce_scatter x2, waiting for transfers between devices: 234 us -> 145 us  [the longest x1 129 us: shards(): lax.psum_scatter(partial_sums, 'col', scatter_dimension=1, tiled=True)]
    all_gather x1, waiting for transfers between devices: 130 us -> 61.8 us  [shards(): hidden_all = lax.all_gather(hidden, 'col', axis=0, tiled=True)]
    pallas_call x0 -> x4, Pallas kernels: none -> 59.4 us  [the longest x1 27.7 us: up_products(): pl.pallas_call(up_kernel, out_shape=jax.ShapeDtypeStruct((2, rows, width)...]
    gather x6 -> x0, local copies, waits for them, and re-layouts: 55.4 us -> none  [the longest x1 23 us: shards(): row_weight = weights_flat[row_assign]]
    dot_general x1, matrix products: 37.7 us -> 0.2 us  [sorted_places(): jnp.einsum('ij,bje->bie', below, per_token.astype(jnp.bfloat16), preferre...]
    convert_element_type x1 -> x0, local copies, waits for them, and re-layouts: 32 us -> none  [shards(): partial_sums.astype(jnp.bfloat16)]
    reshape x1 -> x0, matrix products: 13.3 us -> none  [aligned_apply(): return product.reshape(-1, weights.shape[2])]
    unnamed x17 -> x15, local copies, waits for them, and re-layouts: 4.58 us -> 15.2 us
  transfers between devices with their start and end apart: 4 -> 4, of which waited for: 3 -> 3; matrix products, arithmetic and copies ran while one was open for 11% -> 6% of each run, Pallas kernels for 0% -> 10%
where the time goes in v1:
time: 328 us; the launch traced here: 327 us
  waiting for transfers between devices  207 us (63%)
  Pallas kernels  59.4 us (18%)
  local copies, waits for them, and re-layouts  19.8 us (6%)
  between operations  13.9 us (4%)
  blocking collectives  12.7 us (4%)
  other arithmetic  10.2 us (3%)
  starting transfers between devices  3.69 us (1%)
    reduce_scatter x1, waiting for transfers between devices, shards(): lax.psum_scatter(partial_sums, 'col', scatter_dimension=1, tiled=True)  129 us
    all_gather x1, waiting for transfers between devices, shards(): hidden_all = lax.all_gather(hidden, 'col', axis=0, tiled=True)  61.8 us
    pallas_call x1, Pallas kernels, up_products(): pl.pallas_call(up_kernel, out_shape=jax.ShapeDtypeStruct((2, rows, width)...  27.7 us
    pallas_call x1, Pallas kernels, down_products(): pl.pallas_call(down_kernel, out_shape=jax.ShapeDtypeStruct((count, depth)...  19.7 us
    reduce_scatter x1, waiting for transfers between devices, shards(): mixed = lax.psum_scatter(per_token, 'row', scatter_dimension=0, tiled=True)  16.4 us
    unnamed x15, local copies, waits for them, and re-layouts  15.2 us
    all_gather x1, blocking collectives, shards(): gathered = lax.all_gather(tokens, 'row', axis=0, tiled=True)  12.7 us
    pallas_call x2, Pallas kernels, take_pages(): pl.pallas_call(page_kernel, out_shape=jax.ShapeDtypeStruct(cache.shape, c...  12 us
  transfers between devices with their start and end apart: 4, of which 3 were waited for; matrix products, arithmetic and copies ran while one was open for 6% of the time, Pallas kernels for 10%

profile of v1, /device:TPU:0, one launch (start us, length us, event | category | flops | bytes accessed | tf_op | source)
XLA Modules:
  0.0 326.8 jit_solution(4812247705885396808)
XLA Ops:
  7.2 0.8 convert_reduce_fusion
  8.4 0.6 slice.17
  9.1 0.7 minimum_select_fusion
  9.7 0.7 maximum_select_fusion.low
  10.6 0.2 fusion.3
  10.8 0.8 select_reduce_fusion.1
  11.6 1.1 copy.40
  12.7 12.7 %all_gather.6.tokens = bf16[1024,288]{1,0:T(8,128)(2,1)S(1)} all-gather(bf16[256,288]{1,0:T(8,128)(2,1)S(1)} %copy.40), channel_id=1, replica_groups=mesh['row'=4,'col'=8] {'row'}, dimensions={0}, use_global_device_ids=true | all-gather | bytes 737280 | tf_op jit(solution)/shard_map/all_gather | solution.py:195
  25.3 27.7 %shard_map.113 = bf16[2,2048,1440]{2,1,0:T(8,128)(2,1)} custom-call(s32[15]{0:T(128)S(1)} %get-tuple-element.18.tile, s32[15]{0:T(128)S(1)} %broadcast_minimum_fusion.expert, s32[15]{0:T(128)S(1)} %maximum_select_fusion.low, s32[15]{0:T(128)S(1)} %get-tuple-element.17.high, s32[1,1024]{1,0:T(1,128)S(1)} %get-tuple-element.20.first, ...), custom_call_target="tpu_custom_call" | custom-call | tf_op jit(solution)/shard_map/pallas_call | solution.py:72
  53.1 0.6 copy-done.1
  53.7 0.3 select_reduce_fusion
  54.0 128.7 %reduce-scatter.3.cloned.1.call-done = bf16[2,256,1440]{2,1,0:T(8,128)(2,1)} async-done(((bf16[2,2048,1440]{2,1,0:T(8,128)(2,1)}), bf16[2,256,1440]{2,1,0:T(8,128)(2,1)}) %reduce-scatter.3.cloned.1.call-update) | async-done | bytes 1474576 | tf_op jit(solution)/shard_map/reduce_scatter | solution.py:200
  182.7 1.8 convert_element_type.63
  184.5 1.4 fusion.1
  186.0 0.3 convert_reduce_fusion.2
  186.3 0.1 select_reduce_fusion.4.source
  186.5 0.6 fusion.11
  187.1 1.2 compare_convert_fusion.keep
  188.3 6.1 %shard_map.115 = bf16[2,8,16,2304]{3,2,1,0:T(8,128)(2,1)} custom-call(s32[8]{0:T(128)} %copy-done.3, s32[8]{0:T(128)} %compare_convert_fusion.keep, bf16[2,8,16,2304]{3,2,1,0:T(8,128)(2,1)} %page.1), custom_call_target="tpu_custom_call" | custom-call | tf_op jit(solution)/shard_map/pallas_call | solution.py:142
  194.4 2.4 copy.42
  196.8 3.6 %all-to-all-start = ((bf16[2,8,16,2304]{3,2,0,1:T(8,128)(2,1)}), bf16[2,8,16,2304]{3,2,0,1:T(8,128)(2,1)S(1)}, u32[]{:S(2)}, u32[]{:S(2)}) async-start(bf16[2,8,16,2304]{3,2,0,1:T(8,128)(2,1)} %copy.42), calls=%async_computation.2 | async-start | bytes 2359296 | tf_op jit(solution)/shard_map/all_to_all | solution.py:169
  200.4 0.2 copy.45.first
  200.7 0.2 copy.46.second
  200.9 11.3 %copy.41.weight = bf16[8,1440,288]{2,1,0:T(8,128)(2,1)} copy(bf16[8,1440,288]{1,2,0:T(8,128)(2,1)} %param.13) | data formatting | bytes 13271040 | tf_op args[3]
  212.2 61.8 %all-gather.2.cloned.1.call-done.hidden = bf16[2048,1440]{1,0:T(8,128)(2,1)} async-done(((bf16[256,1440]{1,0:T(8,128)(2,1)}), bf16[2048,1440]{1,0:T(8,128)(2,1)}) %all-gather.2.cloned.1.call-update) | async-done | bytes 5898256 | tf_op jit(solution)/shard_map/all_gather | solution.py:207
  274.1 19.7 %shard_map.114 = bf16[1024,288]{1,0:T(8,128)(2,1)} custom-call(s32[15]{0:T(128)S(1)} %get-tuple-element.18.tile, s32[15]{0:T(128)S(1)} %broadcast_minimum_fusion.expert, s32[15]{0:T(128)S(1)} %maximum_select_fusion.low, s32[15]{0:T(128)S(1)} %get-tuple-element.17.high, s32[1024,1]{1,0:T(8,128)S(1)} %copy.45.first, s32[1024,1]{1,0:T(8,128)S(1)} %copy.46.second, ...), custom_call_target="tpu_custom_call" | custom-call | tf_op jit(solution)/shard_map/pallas_call | solution.py:116
  293.8 0.8 select_reduce_fusion.2.source
  294.6 1.1 copy.43.page
  295.6 0.5 ne.59.keep
  296.2 6.0 %shard_map.116 = bf16[2,8,16,2304]{3,2,1,0:T(8,128)(2,1)} custom-call(s32[8]{0:T(128)} %select_reduce_fusion.2.source, s32[8]{0:T(128)} %ne.59.keep, bf16[2,8,16,2304]{3,2,1,0:T(8,128)(2,1)} %copy.43.page), custom_call_target="tpu_custom_call" | custom-call | tf_op jit(solution)/shard_map/pallas_call | solution.py:142
  302.2 16.4 %reduce-scatter.5.cloned.1.call-done = bf16[256,288]{1,0:T(8,128)(2,1)} async-done(((bf16[1024,288]{1,0:T(8,128)(2,1)}), bf16[256,288]{1,0:T(8,128)(2,1)}) %reduce-scatter.5.cloned.1.call-update) | async-done | bytes 147472 | tf_op jit(solution)/shard_map/reduce_scatter | solution.py:209
  318.6 1.7 copy.44
  (35 shorter events, 0.9 us)
Async XLA Ops:
  7.2 175.5 %reduce-scatter.3.cloned.1.call-start = ((), (), s32[]{:S(2)}) async-start(), calls=%async_computation.3 | async-start | bytes 14155776 | tf_op jit(solution)/shard_map/reduce_scatter | solution.py:200
  53.0 0.7 copy-start.1
  53.0 221.1 %all-gather.2.cloned.1.call-start = ((), (), s32[]{:S(2)}) async-start(), calls=%async_computation.4 | async-start | bytes 7077888 | tf_op jit(solution)/shard_map/all_gather | solution.py:207
  184.5 1.4 copy-start
  184.5 1.9 copy-start.4
  186.4 1.9 copy-start.3
  196.8 97.8 %all-to-all-start = ((bf16[2,8,16,2304]{3,2,0,1:T(8,128)(2,1)}), bf16[2,8,16,2304]{3,2,0,1:T(8,128)(2,1)S(1)}, u32[]{:S(2)}, u32[]{:S(2)}) async-start(bf16[2,8,16,2304]{3,2,0,1:T(8,128)(2,1)} %copy.42), calls=%async_computation.2 | async-start | bytes 2359296 | tf_op jit(solution)/shard_map/all_to_all | solution.py:169
  200.4 118.2 %reduce-scatter.5.cloned.1.call-start = ((), (), s32[]{:S(2)}) async-start(), calls=%async_computation.5 | async-start | bytes 983040 | tf_op jit(solution)/shard_map/reduce_scatter | solution.py:209
  212.2 81.6 %copy-start.2 = (s32[1,8,8]{2,1,0:T(8,128)S(1)}, s32[1,8,8]{2,1,0:T(8,128)}, u32[]{:S(2)}) copy-start(s32[1,8,8]{2,1,0:T(8,128)} %param.18) | copy-start | bytes 772
Sparse Core Ops, SparseCore 0:
  53.1 129.5 reduce-scatter.2
  186.0 87.9 all-gather.1
  293.9 24.6 reduce-scatter.4

commit v2 on v1

--- a/solution.py
+++ b/solution.py
@@ -7,6 +7,7 @@
 
 TILE = 256
 VMEM_BYTES = 48 * 1024 * 1024
+CHUNKS = 2
 
 
 def sorted_places(route_ids, experts):
@@ -52,20 +53,23 @@
 
 def up_kernel(tile, expert, low, high, first, second, tokens, gate, up, out):
     s = pl.program_id(0)
-    place = tile[s] * TILE + lax.broadcasted_iota(jnp.int32, (TILE, 1), 0)
-    mask = (place >= low[s]) & (place < high[s])
-    pick = (first[...] == place) | (second[...] == place)
-    rows = jnp.dot(
-        jnp.where(pick, 1.0, 0.0).astype(jnp.bfloat16), tokens[...], preferred_element_type=jnp.float32
-    ).astype(jnp.bfloat16)
-    for i, weight in enumerate((gate, up)):
-        product = jnp.dot(rows, weight[0], preferred_element_type=jnp.float32)
-        out[i] = jnp.where(mask, product, out[i].astype(jnp.float32)).astype(jnp.bfloat16)
+
+    @pl.when(high[s] > low[s])
+    def _():
+        place = tile[s] * TILE + lax.broadcasted_iota(jnp.int32, (TILE, 1), 0)
+        mask = (place >= low[s]) & (place < high[s])
+        pick = (first[...] == place) | (second[...] == place)
+        rows = jnp.dot(
+            jnp.where(pick, 1.0, 0.0).astype(jnp.bfloat16), tokens[...], preferred_element_type=jnp.float32
+        ).astype(jnp.bfloat16)
+        for i, weight in enumerate((gate, up)):
+            product = jnp.dot(rows, weight[0], preferred_element_type=jnp.float32)
+            out[i] = jnp.where(mask, product, out[i].astype(jnp.float32)).astype(jnp.bfloat16)
 
 
 def up_products(table, places, tokens, gate_weight, up_weight):
     count = tokens.shape[0]
-    rows = 2 * count
+    rows = 2 * count // CHUNKS
     _, depth, width = gate_weight.shape
     whole = lambda s, *_: (0, 0)
     weight = pl.BlockSpec((1, depth, width), lambda s, tile, expert, *_: (expert[s], 0, 0))
@@ -85,28 +89,29 @@
             out_specs=pl.BlockSpec((2, TILE, width), lambda s, tile, *_: (0, tile[s], 0)),
         ),
         compiler_params=pltpu.CompilerParams(vmem_limit_bytes=VMEM_BYTES),
+        cost_estimate=pl.CostEstimate(
+            flops=8 * rows * depth * width, bytes_accessed=2 * gate_weight.size * 2, transcendentals=0
+        ),
     )(*table, places[:, 0].reshape(1, -1), places[:, 1].reshape(1, -1), tokens, gate_weight, up_weight)
 
 
-def down_kernel(tile, expert, low, high, first, second, hidden, weight, out, total):
+def down_kernel(tile, expert, low, high, first, second, hidden, weight, total):
     s = pl.program_id(0)
 
     @pl.when(s == 0)
     def _():
         total[...] = jnp.zeros_like(total)
 
-    place = tile[s] * TILE + lax.broadcasted_iota(jnp.int32, (1, TILE), 1)
-    mask = (place >= low[s]) & (place < high[s])
-    place = jnp.where(mask, place, -1)
-    pick = (first[...] == place) | (second[...] == place)
-    product = jnp.dot(hidden[...], weight[0], preferred_element_type=jnp.float32).astype(jnp.bfloat16)
-    total[...] += jnp.dot(
-        jnp.where(pick, 1.0, 0.0).astype(jnp.bfloat16), product, preferred_element_type=jnp.float32
-    )
-
-    @pl.when(s == pl.num_programs(0) - 1)
+    @pl.when(high[s] > low[s])
     def _():
-        out[...] = total[...].astype(jnp.bfloat16)
+        place = tile[s] * TILE + lax.broadcasted_iota(jnp.int32, (1, TILE), 1)
+        mask = (place >= low[s]) & (place < high[s])
+        place = jnp.where(mask, place, -(1 << 30))
+        pick = (first[...] == place) | (second[...] == place)
+        product = jnp.dot(hidden[...], weight[0], preferred_element_type=jnp.float32).astype(jnp.bfloat16)
+        total[...] += jnp.dot(
+            jnp.where(pick, 1.0, 0.0).astype(jnp.bfloat16), product, preferred_element_type=jnp.float32
+        )
 
 
 def down_products(table, places, hidden, down_weight):
@@ -115,7 +120,7 @@
     whole = lambda s, *_: (0, 0)
     return pl.pallas_call(
         down_kernel,
-        out_shape=jax.ShapeDtypeStruct((count, depth), jnp.bfloat16),
+        out_shape=jax.ShapeDtypeStruct((count, depth), jnp.float32),
         grid_spec=pltpu.PrefetchScalarGridSpec(
             num_scalar_prefetch=4,
             grid=(table[0].shape[0],),
@@ -126,9 +131,11 @@
                 pl.BlockSpec((1, width, depth), lambda s, tile, expert, *_: (expert[s], 0, 0)),
             ],
             out_specs=pl.BlockSpec((count, depth), whole),
-            scratch_shapes=[pltpu.VMEM((count, depth), jnp.float32)],
         ),
         compiler_params=pltpu.CompilerParams(vmem_limit_bytes=VMEM_BYTES),
+        cost_estimate=pl.CostEstimate(
+            flops=4 * hidden.size * depth, bytes_accessed=2 * down_weight.size, transcendentals=0
+        ),
     )(*table, places[:, 0:1], places[:, 1:2], hidden, down_weight)
 
 
@@ -148,6 +155,7 @@
             in_specs=[pl.BlockSpec(block, lambda p, source, keep: (0, source[p], 0, 0))],
             out_specs=pl.BlockSpec(block, lambda p, source, keep: (0, p, 0, 0)),
         ),
+        cost_estimate=pl.CostEstimate(flops=0, bytes_accessed=8 * cache.size, transcendentals=0),
     )(source, keep, cache)
 
 
@@ -195,17 +203,32 @@
     gathered = lax.all_gather(tokens, "row", axis=0, tiled=True)
     decode_cache = move_pages(prefill_cache, dest_col, dest_slot, pages_used)
     places, starts, ends = sorted_places(route_ids, gate_weight.shape[0])
-    table = step_table(starts, ends, rows)
-    partial_sums = up_products(table, places, gathered, gate_weight, up_weight)
-    summed = lax.psum_scatter(partial_sums, "col", scatter_dimension=1, tiled=True).astype(jnp.float32)
-    share = summed.shape[1]
+    span = rows // CHUNKS
+    plans = []
+    for chunk in range(CHUNKS):
+        base = chunk * span
+        table = step_table(jnp.clip(starts - base, 0, span), jnp.clip(ends - base, 0, span), span)
+        plans.append((table, places - base))
+    summed = [
+        lax.psum_scatter(
+            up_products(table, local, gathered, gate_weight, up_weight), "col", scatter_dimension=1, tiled=True
+        )
+        for table, local in plans
+    ]
+    share = span // lax.axis_size("col")
     own_rows = lax.axis_index("col") * share + jnp.arange(share, dtype=jnp.int32)
-    own_weight = jnp.sum(
-        jnp.where(own_rows[:, None, None] == places[None], route_weight[None], 0.0), axis=(1, 2)
-    )
-    hidden = (own_weight[:, None] * jax.nn.silu(summed[0]) * summed[1]).astype(jnp.bfloat16)
-    hidden_all = lax.all_gather(hidden, "col", axis=0, tiled=True)
-    per_token = down_products(table, places, hidden_all, down_weight)
+    hidden_all = []
+    for (_, local), halves in zip(plans, summed):
+        own_weight = jnp.sum(
+            jnp.where(own_rows[:, None, None] == local[None], route_weight[None], 0.0), axis=(1, 2)
+        )
+        gate, up = halves[0].astype(jnp.float32), halves[1].astype(jnp.float32)
+        hidden = (own_weight[:, None] * jax.nn.silu(gate) * up).astype(jnp.bfloat16)
+        hidden_all.append(lax.all_gather(hidden, "col", axis=0, tiled=True))
+    totals = [
+        down_products(table, local, hidden, down_weight) for (table, local), hidden in zip(plans, hidden_all)
+    ]
+    per_token = sum(totals).astype(jnp.bfloat16)
     mixed = lax.psum_scatter(per_token, "row", scatter_dimension=0, tiled=True)
     return (mixed, decode_cache)
 

time: 328 us -> 328 us (level)
  waiting for transfers between devices: 207 us -> 191 us
  local copies, waits for them, and re-layouts: 19.8 us -> 27 us
  other arithmetic: 10.2 us -> 14.1 us
  Pallas kernels: 59.4 us -> 62.8 us
    reduce_scatter x1 -> x2, waiting for transfers between devices: 129 us -> 118 us  [shards(): lax.psum_scatter(up_products(table, local, gathered, gate_weight, up_weig...]
    all_gather x1 -> x2, waiting for transfers between devices: 61.8 us -> 57.3 us  [shards(): hidden_all.append(lax.all_gather(hidden, 'col', axis=0, tiled=True))]
    unnamed x15 -> x21, local copies, waits for them, and re-layouts: 15.2 us -> 18.5 us
    pallas_call x1 -> x2, Pallas kernels: 27.7 us -> 30.3 us  [up_products(): pl.pallas_call(up_kernel, out_shape=jax.ShapeDtypeStruct((2, rows, width)...]
    pallas_call x1 -> x2, Pallas kernels: 19.7 us -> 20.5 us  [down_products(): pl.pallas_call(down_kernel, out_shape=jax.ShapeDtypeStruct((count, depth)...]
  transfers between devices with their start and end apart: 4 -> 6, of which waited for: 3 -> 5; matrix products, arithmetic and copies ran while one was open for 6% -> 9% of each run, Pallas kernels for 10% -> 15%
where the time goes in v2:
time: 328 us; the launch traced here: 326 us
  waiting for transfers between devices  191 us (58%)
  Pallas kernels  62.8 us (19%)
  local copies, waits for them, and re-layouts  27 us (8%)
  other arithmetic  14.1 us (4%)
  between operations  14 us (4%)
  blocking collectives  12.7 us (4%)
  starting transfers between devices  4.45 us (1%)
    reduce_scatter x2, waiting for transfers between devices, shards(): lax.psum_scatter(up_products(table, local, gathered, gate_weight, up_weig...  118 us
    all_gather x2, waiting for transfers between devices, shards(): hidden_all.append(lax.all_gather(hidden, 'col', axis=0, tiled=True))  57.3 us
    pallas_call x2, Pallas kernels, up_products(): pl.pallas_call(up_kernel, out_shape=jax.ShapeDtypeStruct((2, rows, width)...  30.3 us
    pallas_call x2, Pallas kernels, down_products(): pl.pallas_call(down_kernel, out_shape=jax.ShapeDtypeStruct((count, depth)...  20.5 us
    unnamed x21, local copies, waits for them, and re-layouts  18.5 us
    reduce_scatter x1, waiting for transfers between devices, shards(): mixed = lax.psum_scatter(per_token, 'row', scatter_dimension=0, tiled=True)  15.5 us
    all_gather x1, blocking collectives, shards(): gathered = lax.all_gather(tokens, 'row', axis=0, tiled=True)  12.7 us
    pallas_call x2, Pallas kernels, take_pages(): pl.pallas_call(page_kernel, out_shape=jax.ShapeDtypeStruct(cache.shape, c...  12 us
  transfers between devices with their start and end apart: 6, of which 5 were waited for; matrix products, arithmetic and copies ran while one was open for 9% of the time, Pallas kernels for 15%

profile of v2, /device:TPU:0, one launch (start us, length us, event | category | flops | bytes accessed | tf_op | source)
XLA Modules:
  0.0 326.4 jit_solution(2661170633023768021)
XLA Ops:
  7.2 0.9 convert_reduce_fusion
  9.4 0.7 minimum_select_fusion.1
  10.0 0.7 maximum_select_fusion.1.low
  11.1 0.8 select_reduce_fusion.2
  12.7 12.7 %all_gather.9.tokens = bf16[1024,288]{1,0:T(8,128)(2,1)S(1)} all-gather(bf16[256,288]{1,0:T(8,128)(2,1)S(1)} %copy.45), channel_id=1, replica_groups=mesh['row'=4,'col'=8] {'row'}, dimensions={0}, use_global_device_ids=true | all-gather | bytes 737280 | tf_op jit(solution)/shard_map/all_gather | solution.py:203
  25.4 14.4 %shard_map.113 = bf16[2,1024,1440]{2,1,0:T(8,128)(2,1)} custom-call(s32[11]{0:T(128)S(1)} %get-tuple-element.31.tile, s32[11]{0:T(128)S(1)} %broadcast_minimum_fusion.1.expert, s32[11]{0:T(128)S(1)} %maximum_select_fusion.1.low, s32[11]{0:T(128)S(1)} %get-tuple-element.30.high, s32[1,1024]{1,0:T(1,128)S(1)} %bitcast.56, s32[1,1024]{1,0:T(1,128)S(1)} %bitcast.55, ...), custom_call_target="tpu_custom_call" | custom-call | flops 3397386240 | bytes 13271040 | tf_op jit(solution)/shard_map/pallas_call | solution.py:76
  40.4 0.7 minimum_select_fusion
  41.1 0.7 maximum_select_fusion.low
  41.8 1.1 slice_reduce_fusion
  42.9 15.9 %shard_map.115 = bf16[2,1024,1440]{2,1,0:T(8,128)(2,1)} custom-call(s32[11]{0:T(128)S(1)} %get-tuple-element.27.tile, s32[11]{0:T(128)S(1)} %broadcast_minimum_fusion.expert, s32[11]{0:T(128)S(1)} %maximum_select_fusion.low, s32[11]{0:T(128)S(1)} %get-tuple-element.26.high, s32[1,1024]{1,0:T(1,128)S(1)} %bitcast.58, s32[1,1024]{1,0:T(1,128)S(1)} %bitcast.57, ...), custom_call_target="tpu_custom_call" | custom-call | flops 3397386240 | bytes 13271040 | tf_op jit(solution)/shard_map/pallas_call | solution.py:76
  59.9 50.2 %reduce-scatter.4.cloned.1.call-done = bf16[2,128,1440]{2,1,0:T(8,128)(2,1)} async-done(((bf16[2,1024,1440]{2,1,0:T(8,128)(2,1)}), bf16[2,128,1440]{2,1,0:T(8,128)(2,1)}) %reduce-scatter.4.cloned.1.call-update) | async-done | bytes 737296 | tf_op jit(solution)/shard_map/reduce_scatter | solution.py:213
  110.1 2.2 fusion.13
  112.3 68.2 %reduce-scatter.6.cloned.1.call-done = bf16[2,128,1440]{2,1,0:T(8,128)(2,1)} async-done(((bf16[2,1024,1440]{2,1,0:T(8,128)(2,1)}), bf16[2,128,1440]{2,1,0:T(8,128)(2,1)}) %reduce-scatter.6.cloned.1.call-update) | async-done | bytes 737296 | tf_op jit(solution)/shard_map/reduce_scatter | solution.py:213
  180.6 2.2 fusion.12
  183.9 1.2 compare_convert_fusion.keep
  185.2 6.0 %shard_map.117 = bf16[2,8,16,2304]{3,2,1,0:T(8,128)(2,1)} custom-call(s32[8]{0:T(128)} %copy-done.7, s32[8]{0:T(128)} %compare_convert_fusion.keep, bf16[2,8,16,2304]{3,2,1,0:T(8,128)(2,1)} %page.1), custom_call_target="tpu_custom_call" | custom-call | bytes 4718592 | tf_op jit(solution)/shard_map/pallas_call | solution.py:149
  191.2 2.4 copy.50
  193.6 4.2 %all-to-all-start = ((bf16[2,8,16,2304]{3,2,0,1:T(8,128)(2,1)}), bf16[2,8,16,2304]{3,2,0,1:T(8,128)(2,1)}, u32[]{:S(2)}, u32[]{:S(2)}) async-start(bf16[2,8,16,2304]{3,2,0,1:T(8,128)(2,1)} %copy.50), calls=%async_computation.3 | async-start | bytes 2359296 | tf_op jit(solution)/shard_map/all_to_all | solution.py:177
  197.9 11.3 %copy.46.weight = bf16[8,1440,288]{2,1,0:T(8,128)(2,1)} copy(bf16[8,1440,288]{1,2,0:T(8,128)(2,1)} %param.13) | data formatting | bytes 13271040 | tf_op args[3]
  209.2 30.1 %all-gather.3.cloned.1.call-done.hidden = bf16[1024,1440]{1,0:T(8,128)(2,1)} async-done(((bf16[128,1440]{1,0:T(8,128)(2,1)}), bf16[1024,1440]{1,0:T(8,128)(2,1)}) %all-gather.3.cloned.1.call-update) | async-done | bytes 2949136 | tf_op jit(solution)/shard_map/all_gather | solution.py:227
  239.3 1.9 copy-done
  241.2 9.6 %shard_map.114 = f32[1024,288]{1,0:T(8,128)S(1)} custom-call(s32[11]{0:T(128)S(1)} %get-tuple-element.31.tile, s32[11]{0:T(128)S(1)} %broadcast_minimum_fusion.1.expert, s32[11]{0:T(128)S(1)} %maximum_select_fusion.1.low, s32[11]{0:T(128)S(1)} %get-tuple-element.30.high, s32[1024,1]{1,0:T(8,128)S(1)} %get-tuple-element.37.first, ...), custom_call_target="tpu_custom_call" | custom-call | flops 1698693120 | bytes 6635520 | tf_op jit(solution)/shard_map/pallas_call | solution.py:121
  250.8 27.2 %all-gather.5.cloned.1.call-done.hidden = bf16[1024,1440]{1,0:T(8,128)(2,1)} async-done(((bf16[128,1440]{1,0:T(8,128)(2,1)}), bf16[1024,1440]{1,0:T(8,128)(2,1)}) %all-gather.5.cloned.1.call-update) | async-done | bytes 2949136 | tf_op jit(solution)/shard_map/all_gather | solution.py:227
  278.0 1.9 copy-done.1
  279.9 1.0 copy-done.2
  281.0 10.9 %shard_map.116 = f32[1024,288]{1,0:T(8,128)S(1)} custom-call(s32[11]{0:T(128)S(1)} %get-tuple-element.27.tile, s32[11]{0:T(128)S(1)} %broadcast_minimum_fusion.expert, s32[11]{0:T(128)S(1)} %maximum_select_fusion.low, s32[11]{0:T(128)S(1)} %get-tuple-element.26.high, s32[1024,1]{1,0:T(8,128)S(1)} %copy-done.2, s32[1024,1]{1,0:T(8,128)S(1)} %get-tuple-element.34.second, ...), custom_call_target="tpu_custom_call" | custom-call | flops 1698693120 | bytes 6635520 | tf_op jit(solution)/shard_map/pallas_call | solution.py:121
  291.9 1.1 add_convert_fusion
  293.0 0.8 select_reduce_fusion.3.source
  293.8 2.4 copy.51.page
  296.7 6.0 %shard_map.118 = bf16[2,8,16,2304]{3,2,1,0:T(8,128)(2,1)} custom-call(s32[8]{0:T(128)} %select_reduce_fusion.3.source, s32[8]{0:T(128)} %ne.108.keep, bf16[2,8,16,2304]{3,2,1,0:T(8,128)(2,1)} %copy.51.page), custom_call_target="tpu_custom_call" | custom-call | bytes 4718592 | tf_op jit(solution)/shard_map/pallas_call | solution.py:149
  302.7 15.5 %reduce-scatter.8.cloned.1.call-done = bf16[256,288]{1,0:T(8,128)(2,1)} async-done(((bf16[1024,288]{1,0:T(8,128)(2,1)}), bf16[256,288]{1,0:T(8,128)(2,1)}) %reduce-scatter.8.cloned.1.call-update) | async-done | bytes 147472 | tf_op jit(solution)/shard_map/reduce_scatter | solution.py:232
  318.1 1.7 copy.52
  (60 shorter events, 6.1 us)
Async XLA Ops:
  7.2 5.4 %copy-start.3 = (bf16[256,288]{0,1:T(8,128)(2,1)S(1)}, bf16[256,288]{0,1:T(8,128)(2,1)}, u32[]{:S(2)}) copy-start(bf16[256,288]{0,1:T(8,128)(2,1)} %param.10) | copy-start | bytes 442372
  7.2 102.9 %reduce-scatter.4.cloned.1.call-start = ((), (), s32[]{:S(2)}) async-start(), calls=%async_computation.4 | async-start | bytes 7077888 | tf_op jit(solution)/shard_map/reduce_scatter | solution.py:213
  39.8 140.8 %reduce-scatter.6.cloned.1.call-start = ((), (), s32[]{:S(2)}) async-start(), calls=%async_computation.6 | async-start | bytes 7077888 | tf_op jit(solution)/shard_map/reduce_scatter | solution.py:213
  58.8 0.7 copy-start.5
  58.8 180.5 %all-gather.3.cloned.1.call-start = ((), (), s32[]{:S(2)}) async-start(), calls=%async_computation.5 | async-start | bytes 3538944 | tf_op jit(solution)/shard_map/all_gather | solution.py:227
  110.1 72.7 %copy-start.4 = (s32[1,8,8]{2,1,0:T(8,128)S(1)}, s32[1,8,8]{2,1,0:T(8,128)}, u32[]{:S(2)}) copy-start(s32[1,8,8]{2,1,0:T(8,128)} %param.17) | copy-start | bytes 772
  110.1 73.2 %copy-start.8 = (s32[1,8]{1,0:T(1,128)S(1)}, s32[1,8]{1,0:T(1,128)}, u32[]{:S(2)}) copy-start(s32[1,8]{1,0:T(1,128)} %param.19) | copy-start | bytes 100
  112.3 165.7 %all-gather.5.cloned.1.call-start = ((), (), s32[]{:S(2)}) async-start(), calls=%async_computation.7 | async-start | bytes 3538944 | tf_op jit(solution)/shard_map/all_gather | solution.py:227
  183.3 1.9 copy-start.7
  193.6 100.2 %all-to-all-start = ((bf16[2,8,16,2304]{3,2,0,1:T(8,128)(2,1)}), bf16[2,8,16,2304]{3,2,0,1:T(8,128)(2,1)}, u32[]{:S(2)}, u32[]{:S(2)}) async-start(bf16[2,8,16,2304]{3,2,0,1:T(8,128)(2,1)} %copy.50), calls=%async_computation.3 | async-start | bytes 2359296 | tf_op jit(solution)/shard_map/all_to_all | solution.py:177
  197.8 120.3 %reduce-scatter.8.cloned.1.call-start = ((), (), s32[]{:S(2)}) async-start(), calls=%async_computation.8 | async-start | bytes 983040 | tf_op jit(solution)/shard_map/reduce_scatter | solution.py:232
  239.3 1.9 copy-start
  278.0 1.9 copy-start.1
  279.9 1.0 copy-start.2
  291.9 1.2 copy-start.6
Sparse Core Ops, SparseCore 0:
  39.9 70.0 reduce-scatter.3
  112.4 68.1 reduce-scatter.5
  182.2 57.0 all-gather.2
  240.8 37.1 all-gather.4
  293.1 24.9 reduce-scatter.7
